TPU v7x, 256 devices: a whole 4x4x8 slice. The times are simulated.
256 devices in a mesh: pb: 32 (over z_lo, y, x), wa: 8 (over z_hi, core).
Axes of the slice: x: 4, y: 4, z: 8 (z_hi: 4, z_lo: 2; z = z_hi * 2 + z_lo), core: 2. Of those that a mesh axis runs over, the one named last changes fastest.
Arguments:
- propagator: bfloat16 [80, 4096], P(None, 'pb'), may hold values from -6 to 6
- vertex: bfloat16 [256, 16, 57600], P('pb', 'wa'), may hold values from -0.005859375 to 0.005859375
- momentum_shift: int32 [256, 4096], P('pb'), may hold values from 0 to 4095, as said below
- frequency_shift: int32 [16, 48], P('wa'), may hold values from 0 to 79, as said below
Outputs:
- flow: float32 [48, 4096], P('wa', 'pb')
Inputs may be any that keep to these rules, and one draw needn't show every extreme that they name: momentum_shift[q, k] is x * 64 + y for the lattice momentum k shifted by the q-th transfer momentum of the window, periodic on the 64 x 64 lattice; every row is a permutation, and the 256 transfer momenta are distinct. frequency_shift[w, m] = m + o_w, where the bosonic offsets o_w are distinct, increasing in w, with o_0 = 0 and the last one 32.
All inputs are finite; a program needn't handle non-finite values.
Results may differ from a plain program's by a relative error of at most 0.0025.
Values may be sent and summed in bfloat16 or wider, within the bound.
A program may use at most 64 MiB of HBM per device.

v0:
```python
import math

import jax
import jax.numpy as jnp
from jax import lax
from jax.sharding import PartitionSpec as P

LAT = 64
NFF = 5
NF = 48
NB = 240


def form_factors(momenta):
    angle_x = (momenta // LAT).astype(jnp.float32) * (2.0 * math.pi / LAT)
    angle_y = (momenta % LAT).astype(jnp.float32) * (2.0 * math.pi / LAT)
    root_two = math.sqrt(2.0)
    return jnp.stack(
        [
            jnp.ones_like(angle_x),
            root_two * jnp.cos(angle_x),
            root_two * jnp.cos(angle_y),
            root_two * jnp.sin(angle_x),
            root_two * jnp.sin(angle_y),
        ]
    )


def pair_flow(propagator, block, shift_row, frequency_row, factors):
    selected = jnp.take(propagator, frequency_row, axis=0)
    shifted = jnp.take(selected, shift_row, axis=1).astype(jnp.float32)
    projected = (
        (factors[:, None, :] * shifted[None, :, :]).reshape(NFF * NF, -1).astype(jnp.bfloat16)
    )
    contracted = jnp.dot(block.reshape(NB, NB), projected, preferred_element_type=jnp.float32)
    return jnp.sum(factors[:, None, :] * contracted.reshape(NFF, NF, -1), axis=0)


def local(propagator, vertex, momentum_shift, frequency_shift):
    gathered = lax.all_gather(propagator, "pb", axis=1, tiled=True)
    groups = lax.axis_size("pb")
    width_local = propagator.shape[1]
    local_momenta = vertex.shape[0]
    local_bosons = vertex.shape[1]
    freq_count = frequency_shift.shape[1]
    rows_each = freq_count // lax.axis_size("wa")
    row_count = rows_each * lax.axis_size(("pb", "wa"))
    offset_most = freq_count - rows_each
    block_count = min((offset_most + row_count - 1) // freq_count + 1, groups)
    first_block = jnp.minimum(jnp.int32(0) // freq_count, groups - block_count)
    column_count = block_count * width_local
    first_column = first_block * width_local
    momenta = first_column + jnp.arange(column_count, dtype=jnp.int32)
    factors = form_factors(momenta)

    def accumulate(pair_index, total):
        q_index = pair_index // local_bosons
        w_index = pair_index % local_bosons
        shift_row = momentum_shift[q_index]
        term = pair_flow(
            gathered, vertex[q_index, w_index], shift_row, frequency_shift[w_index], factors
        )
        return total + term

    total = lax.fori_loop(
        0,
        local_momenta * local_bosons,
        accumulate,
        jnp.zeros((freq_count, column_count), jnp.float32),
    )
    blocks = (-total).reshape(freq_count, block_count, width_local).transpose(1, 0, 2)
    blocks = blocks.reshape(block_count * freq_count, width_local)
    return lax.psum_scatter(blocks, ("pb", "wa"), scatter_dimension=0, tiled=True)


def solution(mesh):
    in_specs = (P(None, "pb"), P("pb", "wa", None), P("pb", None), P("wa", None))
    out_specs = P("wa", "pb")
    return jax.shard_map(local, mesh=mesh, in_specs=in_specs, out_specs=out_specs, check_vma=False)
```

profile of v0, /device:TPU:1, one launch (start us, length us, event | category | flops | bytes accessed | tf_op | source)
XLA Modules:
  0.0 830.6 jit_solution(8188016657167088095)
XLA Ops:
  8.3 72.7 %all_gather.3 = bf16[80,4096]{1,0:T(8,128)(2,1)S(1)} all-gather(bf16[80,128]{1,0:T(8,128)(2,1)} %param.6), channel_id=1, replica_groups=mesh['pb'=32,'wa'=8] {'pb'}, dimensions={1}, use_global_device_ids=true | all-gather | bytes 675840 | tf_op jit(solution)/shard_map/all_gather | solution.py:40
  81.8 474.8 %while.16 = (s32[]{:T(128)}, f32[48,4096]{1,0:T(8,128)}, f32[5,4096]{1,0:T(8,128)}, bf16[8,2,57600]{2,1,0:T(2,128)(2,1)}, s32[8,4096]{1,0:T(8,128)}, /*index=5*/...) while((s32[]{:T(128)}, f32[48,4096]{1,0:T(8,128)}, ...), condition=%wide.region_2.3_spmd.clone, body=%wide.region_0.2_spmd.clone.sunk | while | flops 476620224 | bytes 14960034 | solution.py:65
  84.9 15.0 %gather_fusion.1 = bf16[4096,48]{1,0:T(8,128)(2,1)} fusion(bf16[48,4096]{0,1:T(8,128)(2,1)S(1)} %copy.18, s32[4096]{0:T(1024)S(1)} %broadcast_clamp_fusion.2), kind=kCustom, calls=%fused_computation.1.clone.clone.1 | custom fusion | bytes 802816 | tf_op jit(solution)/shard_map/while/body/eval_jaxpr/jit(_take)/gather | solution.py:31
  99.9 3.4 convert_bitcast_fusion.2
  113.5 15.0 %gather_fusion.1 = bf16[4096,48]{1,0:T(8,128)(2,1)} fusion(bf16[48,4096]{0,1:T(8,128)(2,1)S(1)} %copy.18, s32[4096]{0:T(1024)S(1)} %broadcast_clamp_fusion.2), kind=kCustom, calls=%fused_computation.1.clone.clone.1 | custom fusion | bytes 802816 | tf_op jit(solution)/shard_map/while/body/eval_jaxpr/jit(_take)/gather | solution.py:31
  128.5 3.4 convert_bitcast_fusion.2
  138.0 2.1 select_add_fusion.2
  143.3 15.0 %gather_fusion.1 = bf16[4096,48]{1,0:T(8,128)(2,1)} fusion(bf16[48,4096]{0,1:T(8,128)(2,1)S(1)} %copy.18, s32[4096]{0:T(1024)S(1)} %broadcast_clamp_fusion.2), kind=kCustom, calls=%fused_computation.1.clone.clone.1 | custom fusion | bytes 802816 | tf_op jit(solution)/shard_map/while/body/eval_jaxpr/jit(_take)/gather | solution.py:31
  158.3 3.4 convert_bitcast_fusion.2
  167.7 2.1 select_add_fusion.2
  173.0 15.0 %gather_fusion.1 = bf16[4096,48]{1,0:T(8,128)(2,1)} fusion(bf16[48,4096]{0,1:T(8,128)(2,1)S(1)} %copy.18, s32[4096]{0:T(1024)S(1)} %broadcast_clamp_fusion.2), kind=kCustom, calls=%fused_computation.1.clone.clone.1 | custom fusion | bytes 802816 | tf_op jit(solution)/shard_map/while/body/eval_jaxpr/jit(_take)/gather | solution.py:31
  188.0 3.4 convert_bitcast_fusion.2
  197.5 2.1 select_add_fusion.2
  202.8 15.0 %gather_fusion.1 = bf16[4096,48]{1,0:T(8,128)(2,1)} fusion(bf16[48,4096]{0,1:T(8,128)(2,1)S(1)} %copy.18, s32[4096]{0:T(1024)S(1)} %broadcast_clamp_fusion.2), kind=kCustom, calls=%fused_computation.1.clone.clone.1 | custom fusion | bytes 802816 | tf_op jit(solution)/shard_map/while/body/eval_jaxpr/jit(_take)/gather | solution.py:31
  217.8 3.4 convert_bitcast_fusion.2
  227.2 2.1 select_add_fusion.2
  232.5 15.0 %gather_fusion.1 = bf16[4096,48]{1,0:T(8,128)(2,1)} fusion(bf16[48,4096]{0,1:T(8,128)(2,1)S(1)} %copy.18, s32[4096]{0:T(1024)S(1)} %broadcast_clamp_fusion.2), kind=kCustom, calls=%fused_computation.1.clone.clone.1 | custom fusion | bytes 802816 | tf_op jit(solution)/shard_map/while/body/eval_jaxpr/jit(_take)/gather | solution.py:31
  247.5 3.4 convert_bitcast_fusion.2
  257.0 2.1 select_add_fusion.2
  262.3 15.0 %gather_fusion.1 = bf16[4096,48]{1,0:T(8,128)(2,1)} fusion(bf16[48,4096]{0,1:T(8,128)(2,1)S(1)} %copy.18, s32[4096]{0:T(1024)S(1)} %broadcast_clamp_fusion.2), kind=kCustom, calls=%fused_computation.1.clone.clone.1 | custom fusion | bytes 802816 | tf_op jit(solution)/shard_map/while/body/eval_jaxpr/jit(_take)/gather | solution.py:31
  277.3 3.4 convert_bitcast_fusion.2
  286.7 2.1 select_add_fusion.2
  292.0 15.0 %gather_fusion.1 = bf16[4096,48]{1,0:T(8,128)(2,1)} fusion(bf16[48,4096]{0,1:T(8,128)(2,1)S(1)} %copy.18, s32[4096]{0:T(1024)S(1)} %broadcast_clamp_fusion.2), kind=kCustom, calls=%fused_computation.1.clone.clone.1 | custom fusion | bytes 802816 | tf_op jit(solution)/shard_map/while/body/eval_jaxpr/jit(_take)/gather | solution.py:31
  307.1 3.4 convert_bitcast_fusion.2
  316.5 2.1 select_add_fusion.2
  321.8 15.0 %gather_fusion.1 = bf16[4096,48]{1,0:T(8,128)(2,1)} fusion(bf16[48,4096]{0,1:T(8,128)(2,1)S(1)} %copy.18, s32[4096]{0:T(1024)S(1)} %broadcast_clamp_fusion.2), kind=kCustom, calls=%fused_computation.1.clone.clone.1 | custom fusion | bytes 802816 | tf_op jit(solution)/shard_map/while/body/eval_jaxpr/jit(_take)/gather | solution.py:31
  336.8 3.4 convert_bitcast_fusion.2
  346.2 2.1 select_add_fusion.2
  351.5 15.0 %gather_fusion.1 = bf16[4096,48]{1,0:T(8,128)(2,1)} fusion(bf16[48,4096]{0,1:T(8,128)(2,1)S(1)} %copy.18, s32[4096]{0:T(1024)S(1)} %broadcast_clamp_fusion.2), kind=kCustom, calls=%fused_computation.1.clone.clone.1 | custom fusion | bytes 802816 | tf_op jit(solution)/shard_map/while/body/eval_jaxpr/jit(_take)/gather | solution.py:31
  366.6 3.4 convert_bitcast_fusion.2
  376.0 2.1 select_add_fusion.2
  381.3 15.0 %gather_fusion.1 = bf16[4096,48]{1,0:T(8,128)(2,1)} fusion(bf16[48,4096]{0,1:T(8,128)(2,1)S(1)} %copy.18, s32[4096]{0:T(1024)S(1)} %broadcast_clamp_fusion.2), kind=kCustom, calls=%fused_computation.1.clone.clone.1 | custom fusion | bytes 802816 | tf_op jit(solution)/shard_map/while/body/eval_jaxpr/jit(_take)/gather | solution.py:31
  396.3 3.4 convert_bitcast_fusion.2
  405.7 2.1 select_add_fusion.2
  411.0 15.0 %gather_fusion.1 = bf16[4096,48]{1,0:T(8,128)(2,1)} fusion(bf16[48,4096]{0,1:T(8,128)(2,1)S(1)} %copy.18, s32[4096]{0:T(1024)S(1)} %broadcast_clamp_fusion.2), kind=kCustom, calls=%fused_computation.1.clone.clone.1 | custom fusion | bytes 802816 | tf_op jit(solution)/shard_map/while/body/eval_jaxpr/jit(_take)/gather | solution.py:31
  426.0 3.4 convert_bitcast_fusion.2
  435.5 2.1 select_add_fusion.2
  440.8 15.0 %gather_fusion.1 = bf16[4096,48]{1,0:T(8,128)(2,1)} fusion(bf16[48,4096]{0,1:T(8,128)(2,1)S(1)} %copy.18, s32[4096]{0:T(1024)S(1)} %broadcast_clamp_fusion.2), kind=kCustom, calls=%fused_computation.1.clone.clone.1 | custom fusion | bytes 802816 | tf_op jit(solution)/shard_map/while/body/eval_jaxpr/jit(_take)/gather | solution.py:31
  455.8 3.4 convert_bitcast_fusion.2
  465.2 2.1 select_add_fusion.2
  470.5 15.0 %gather_fusion.1 = bf16[4096,48]{1,0:T(8,128)(2,1)} fusion(bf16[48,4096]{0,1:T(8,128)(2,1)S(1)} %copy.18, s32[4096]{0:T(1024)S(1)} %broadcast_clamp_fusion.2), kind=kCustom, calls=%fused_computation.1.clone.clone.1 | custom fusion | bytes 802816 | tf_op jit(solution)/shard_map/while/body/eval_jaxpr/jit(_take)/gather | solution.py:31
  485.5 3.4 convert_bitcast_fusion.2
  500.3 15.0 %gather_fusion.1 = bf16[4096,48]{1,0:T(8,128)(2,1)} fusion(bf16[48,4096]{0,1:T(8,128)(2,1)S(1)} %copy.18, s32[4096]{0:T(1024)S(1)} %broadcast_clamp_fusion.2), kind=kCustom, calls=%fused_computation.1.clone.clone.1 | custom fusion | bytes 802816 | tf_op jit(solution)/shard_map/while/body/eval_jaxpr/jit(_take)/gather | solution.py:31
  515.3 3.4 convert_bitcast_fusion.2
  524.7 2.1 select_add_fusion.2
  530.0 15.0 %gather_fusion.1 = bf16[4096,48]{1,0:T(8,128)(2,1)} fusion(bf16[48,4096]{0,1:T(8,128)(2,1)S(1)} %copy.18, s32[4096]{0:T(1024)S(1)} %broadcast_clamp_fusion.2), kind=kCustom, calls=%fused_computation.1.clone.clone.1 | custom fusion | bytes 802816 | tf_op jit(solution)/shard_map/while/body/eval_jaxpr/jit(_take)/gather | solution.py:31
  545.0 3.4 convert_bitcast_fusion.2
  558.7 263.8 %all-reduce.3.cloned.1.call-done = f32[1536,128]{1,0:T(8,128)} async-done(((f32[1536,128]{1,0:T(8,128)}), f32[1536,128]{1,0:T(8,128)}) %all-reduce.3.cloned.1.call-update) | async-done | bytes 786448
  (300 shorter events, 157.1 us)
Async XLA Ops:
  6.5 815.9 %all-reduce.3.cloned.1.call-start = ((), (), s32[]{:S(2)}) async-start(), calls=%async_computation | async-start | bytes 1572864
  81.8 1.6 copy-start.1
  103.9 3.8 copy-start
  110.4 1.6 copy-start.1
  132.5 3.8 copy-start
  140.1 1.6 copy-start.1
  162.3 3.8 copy-start
  169.9 1.6 copy-start.1
  192.0 3.8 copy-start
  199.6 1.6 copy-start.1
  221.8 3.8 copy-start
  229.4 1.6 copy-start.1
  251.5 3.8 copy-start
  259.1 1.6 copy-start.1
  281.3 3.8 copy-start
  288.9 1.6 copy-start.1
  311.0 3.8 copy-start
  318.6 1.6 copy-start.1
  340.8 3.8 copy-start
  348.4 1.6 copy-start.1
  370.5 3.8 copy-start
  378.1 1.6 copy-start.1
  400.3 3.8 copy-start
  407.9 1.6 copy-start.1
  430.0 3.8 copy-start
  437.6 1.6 copy-start.1
  459.7 3.8 copy-start
  467.4 1.6 copy-start.1
  489.5 3.8 copy-start
  497.1 1.6 copy-start.1
  519.2 3.8 copy-start
  526.8 1.6 copy-start.1
  549.0 3.8 copy-start
Sparse Core Ops, SparseCore 0:
  558.8 263.6 all-reduce.2
where the time goes:
time: 835 us; the launch traced here: 831 us
  local copies, waits for them, and re-layouts  312 us (37%)
  waiting for transfers between devices  264 us (32%)
  other arithmetic  141 us (17%)
  blocking collectives  72.7 us (9%)
  matrix products  26.1 us (3%)
  between operations  13.4 us (2%)
    unnamed x2, waiting for transfers between devices  264 us
    gather x16, local copies, waits for them, and re-layouts, pair_flow(): shifted = jnp.take(selected, shift_row, axis=1).astype(jnp.float32)  240 us
    all_gather x1, blocking collectives, local(): gathered = lax.all_gather(propagator, 'pb', axis=1, tiled=True)  72.7 us
    convert_element_type x16, other arithmetic, pair_flow(): shifted = jnp.take(selected, shift_row, axis=1).astype(jnp.float32)  53.9 us
    add x16, other arithmetic, accumulate(): return total + term  33.1 us
    dynamic_slice x16, local copies, waits for them, and re-layouts, accumulate(): vertex[q_index, w_index]  26.1 us
    dot_general x16, matrix products, pair_flow(): jnp.dot(block.reshape(NB, NB), projected, preferred_element_type=jnp.floa...  26.1 us
    convert_element_type x16, other arithmetic, pair_flow(): (factors[:, None, :] * shifted[None, :, :]).reshape(NFF * NF, -1)  20.5 us
  transfers between devices with their start and end apart: 1, of which 1 were waited for; matrix products, arithmetic and copies ran while one was open for 0% of the time, Pallas kernels for 0%

commit v1 on v0

v1 whole, which is shorter than its diff:
```python
import math

import jax
import jax.numpy as jnp
import numpy as np
from jax import lax
from jax.experimental import pallas as pl
from jax.experimental.pallas import tpu as pltpu

LAT = 64
F32 = jnp.float32
BF16 = jnp.bfloat16
I32 = jnp.int32
NQ = 8
NB = 13
ROWS = 320
KQ = 128
STEPS = 16

BLOCKS = (
    ((0, 0, 1), (1, 1, 1), (2, 2, 1), (3, 3, 1), (4, 4, 1)),
    ((0, 1, 1), (1, 0, 1)),
    ((0, 2, 1), (2, 0, 1)),
    ((0, 3, 1), (3, 0, 1)),
    ((0, 4, 1), (4, 0, 1)),
    ((1, 1, 1), (3, 3, -1)),
    ((1, 3, 1), (3, 1, 1)),
    ((2, 2, 1), (4, 4, -1)),
    ((2, 4, 1), (4, 2, 1)),
    ((1, 2, 1), (2, 1, 1)),
    ((1, 4, 1), (4, 1, 1)),
    ((2, 3, 1), (3, 2, 1)),
    ((3, 4, 1), (4, 3, 1)),
)


def minus_functions():
    k = np.arange(LAT * LAT)
    a = (k // LAT) * (2.0 * math.pi / LAT)
    b = (k % LAT) * (2.0 * math.pi / LAT)
    root = math.sqrt(2.0)
    ca, cb, sa, sb = np.cos(a), np.cos(b), np.sin(a), np.sin(b)
    rows = [
        np.ones_like(a),
        root * ca,
        root * cb,
        root * sa,
        root * sb,
        np.cos(2 * a),
        np.sin(2 * a),
        np.cos(2 * b),
        np.sin(2 * b),
        2 * ca * cb,
        2 * ca * sb,
        2 * cb * sa,
        2 * sa * sb,
    ]
    table = np.zeros((16, LAT * LAT), np.float32)
    table[:NB] = -np.stack(rows)
    return np.ascontiguousarray(table.reshape(16, 32, 128).transpose(1, 0, 2))


def kernel(
    prop, vert, mom, freq, table, out,
    vb, s32, wown, wrecv, lhs, gs, dup, rhs0, rhs1, tab, momv, freqv,
    ssend, srecv, red, fsend, frecv, whole,
    in_sem, v_sem, ag_s, ag_r, z_s, z_r, c_s, c_r, c2_s, c2_r, w_s, w_r, s_s, s_r, f_s, f_r,
):
    p = lax.axis_index("pb")
    wa = lax.axis_index("wa")
    zl = p // 16
    yy = (p // 4) % 4
    xx = p % 4
    core = wa % 2
    z = (wa // 2) * 2 + zl

    def plane(e, sign):
        ey = e // 4
        ex = e % 4
        return ((yy + sign * ey + 4) % 4) * 4 + (xx + sign * ex + 4) % 4

    def column(dz, dc):
        zz = (z + dz) % 8
        return ((zz % 2) * 16 + p % 16, (zz // 2) * 2 + (core + dc) % 2)

    def remote(src, dst, send, recv, device):
        return pltpu.make_async_remote_copy(
            src_ref=src, dst_ref=dst, send_sem=send, recv_sem=recv,
            device_id=device, device_id_type=pl.DeviceIdType.MESH,
        )

    def each(n, body):
        def step(i, carry):
            body(i)
            return carry

        lax.fori_loop(0, n, step, 0)

    c_mom = pltpu.make_async_copy(mom.at[:, pl.ds(0, 128)], momv, in_sem.at[0])
    c_freq = pltpu.make_async_copy(freq, freqv, in_sem.at[1])
    c_tab = pltpu.make_async_copy(table, tab, in_sem.at[2])
    c_own = pltpu.make_async_copy(prop, gs.at[p], in_sem.at[3])
    c_mom.start()
    c_freq.start()

    def piece(i):
        rows = pl.ds(pl.multiple_of(i * 800, 800), 800)
        return pltpu.make_async_copy(vert.at[rows], vb.at[rows], v_sem.at[i])

    each(9, lambda i: piece(i).start())
    c_own.start()
    c_tab.start()

    barrier = pltpu.get_barrier_semaphore()

    def greet(i):
        e = i + 1
        pl.semaphore_signal(
            barrier, inc=1, device_id=(zl * 16 + plane(e, 1), wa), device_id_type=pl.DeviceIdType.MESH
        )
        pl.semaphore_signal(
            barrier, inc=1, device_id=column(e // 2, e % 2), device_id_type=pl.DeviceIdType.MESH
        )

    each(15, greet)

    def widen(i):
        piece(i).wait()
        for t in range(5):
            rows = pl.ds(pl.multiple_of(i * 800 + t * 160, 160), 160)
            s32[rows, :] = vb[rows, :].astype(F32)

    each(9, widen)
    s32[pl.ds(7200, 64), :] = jnp.zeros((64, 128), F32)

    def clear(q):
        for half in range(2):
            wown[half, q, pl.ds(312, 8), :] = jnp.zeros((8, 128), F32)
        for r in (rhs0, rhs1):
            r[pl.ds(pl.multiple_of(q * KQ + 80, 16), KQ - 80), :] = jnp.zeros((KQ - 80, 256), BF16)

    each(NQ, clear)
    c_mom.wait()
    c_freq.wait()
    pl.semaphore_wait(barrier, 30)

    def item(i):
        return 2 * i + core

    def ag(i):
        e = item(i)
        return remote(prop, gs.at[p], ag_s.at[i], ag_r.at[i], (zl * 16 + plane(e, 1), wa))

    up = 1 + 6 * core

    def own_slot(i):
        return zl * 16 + plane(item(i), -1)

    def far_slot(i):
        return (1 - zl) * 16 + plane(item(i), -1)

    def zf(i):
        slot = own_slot(i)
        return remote(gs.at[slot], gs.at[slot], z_s.at[i], z_r.at[i], column(up, 0))

    def cf(i):
        slot = own_slot(i)
        return remote(gs.at[slot], gs.at[slot], c_s.at[i], c_r.at[i], column(0, 1))

    def cf2(i):
        slot = far_slot(i)
        return remote(gs.at[slot], gs.at[slot], c2_s.at[i], c2_r.at[i], column(0, 1))

    def start_ag(i):
        @pl.when(item(i) != 0)
        def _():
            ag(i).start()

    each(8, start_ag)
    c_own.wait()

    def pass_on(i):
        @pl.when(item(i) != 0)
        def _():
            ag(i).wait_recv()
            cf(i).start()

        zf(i).start()

    def pass_on_far(i):
        zf(i).wait_recv()
        cf2(i).start()

    lane = lax.broadcasted_iota(I32, (8, 128), 1)

    def w_send(q):
        return remote(wown.at[1 - core, q], wrecv.at[q], w_s.at[q], w_r.at[q], column(0, 1))

    def prepare(q):
        shifts = [freqv[w, 0] for w in range(2)]
        valid = [(lane >= o) & (lane < o + 48) for o in shifts]
        for i in range(8):
            total = [None] * NB
            for w in range(2):
                blocks = {}
                for n2 in range(5):
                    off = 240 * i + 48 * n2
                    s, start = off // 128, off % 128
                    amount = (shifts[w] + (128 - start)) % 128
                    for n in range(5):
                        row = q * 900 + 180 * n + w + 2 * s
                        value = s32[pl.ds(row, 8, stride=30), :]
                        if start > 80:
                            after = s32[pl.ds(row + 2, 8, stride=30), :]
                            value = jnp.where(lane < start, after, value)
                        blocks[n, n2] = pltpu.roll(value, amount, 1)
                for f in range(NB):
                    term = None
                    for n, n2, sign in BLOCKS[f]:
                        if term is None:
                            term = blocks[n, n2]
                        elif sign > 0:
                            term = term + blocks[n, n2]
                        else:
                            term = term - blocks[n, n2]
                    term = jnp.where(valid[w], term, 0.0)
                    total[f] = term if total[f] is None else total[f] + term
            for f in range(NB):
                wown[i // 4, q, pl.ds(24 * f + 6 * (i % 4), 6), :] = total[f][0:6]
        w_send(q).start()
        pass_on(q)

    each(NQ, prepare)
    each(8, pass_on_far)

    def settle(i):
        e = 2 * i + (1 - core)
        near = zl * 16 + plane(e, -1)
        far = (1 - zl) * 16 + plane(e, -1)

        @pl.when(e != 0)
        def _():
            remote(gs.at[near], gs.at[near], c_s.at[i], c_r.at[i], column(0, 1)).wait_recv()

        remote(gs.at[far], gs.at[far], c2_s.at[i], c2_r.at[i], column(0, 1)).wait_recv()

    each(8, settle)

    low = lax.broadcasted_iota(I32, (80, 128), 1) < 64

    def double(b):
        value = gs[b]
        turned = pltpu.roll(value, 64, 1)
        dup[2 * b] = jnp.where(low, value, turned)
        dup[2 * b + 1] = jnp.where(low, turned, value)

    each(32, double)

    for q in range(NQ):
        w_send(q).wait_recv()
        lhs[:, KQ * q : KQ * (q + 1)] = (wown[core, q] + wrecv[q]).astype(BF16)
    c_tab.wait()

    def build(step, ref):
        block = plane(15 - step, 1)
        for q in range(NQ):
            shift = momv[q, 0]
            qx = shift // 64
            amount = (128 - shift % 64) % 128
            for half in range(2):
                x = 2 * (block + 16 * half) + qx
                first = pltpu.roll(dup[x % 64], amount, 1)
                second = pltpu.roll(dup[(x + 1) % 64], amount, 1)
                ref[KQ * q : KQ * q + 80, 128 * half : 128 * half + 128] = jnp.where(low, first, second)

    def s_copy(e):
        return remote(ssend.at[e], srecv.at[e], s_s.at[e], s_r.at[e], (zl * 16 + plane(e, 1), wa))

    def contract(step, ref):
        e = 15 - step
        block = plane(e, 1)
        acc = jnp.dot(lhs[...], ref[...], preferred_element_type=F32)
        for half in range(2):
            factors = tab[block + 16 * half]
            flow = None
            for f in range(NB):
                term = factors[f : f + 1, :] * acc[24 * f : 24 * f + 24, 128 * half : 128 * half + 128]
                flow = term if flow is None else flow + term
            ssend[e, half] = flow

        @pl.when(e != 0)
        def _():
            s_copy(e).start()

    build(0, rhs0)

    def two(i):
        build(2 * i + 1, rhs1)
        contract(2 * i, rhs0)
        build((2 * i + 2) % STEPS, rhs0)
        contract(2 * i + 1, rhs1)

    each(STEPS // 2, two)

    red[...] = ssend[0]

    def gather_sum(i):
        e = 15 - i
        s_copy(e).wait_recv()
        red[...] += srecv[e]

    each(15, gather_sum)

    for zt in range(2):
        for h in range(4):
            first = 3 * (h // 2) + h % 2
            for a in range(2):
                fsend[zt * 4 + h, 4 * a : 4 * a + 4, :] = red[zt, pl.ds(first + a, 4, stride=6), :]

    def f_copy(d):
        zz = (z + d // 2) % 8
        return remote(
            fsend.at[(zz % 2) * 4 + zz // 2], frecv.at[d], f_s.at[d], f_r.at[d], column(d // 2, d % 2)
        )

    each(15, lambda i: f_copy(15 - i).start())
    same = fsend[zl * 4 + z // 2]
    other = jnp.zeros((8, 128), F32)
    for d in range(15, 0, -1):
        f_copy(d).wait_recv()
        if d % 2 == 0:
            same = same + frecv[d]
        else:
            other = other + frecv[d]
    zero = core == 0
    one = jnp.where(zero, same, other)
    two_ = jnp.where(zero, other, same)
    whole[0:4, :] = one[0:4]
    whole[4:8, :] = two_[0:4]
    whole[8:12, :] = one[4:8]
    whole[12:16, :] = two_[4:8]
    out[...] = whole[pl.ds(6 * core + 4 * ((z // 2) % 2), 6), :]

    def drain(i):
        @pl.when(item(i) != 0)
        def _():
            ag(i).wait_send()
            cf(i).wait_send()

        zf(i).wait_send()
        cf2(i).wait_send()
        w_send(i).wait_send()

    each(8, drain)

    def drain_sums(i):
        s_copy(i + 1).wait_send()
        f_copy(i + 1).wait_send()

    each(15, drain_sums)


def local(propagator, vertex, momentum_shift, frequency_shift):
    rows = vertex.transpose(0, 2, 1).reshape(3600, 128, 2).transpose(0, 2, 1).reshape(7200, 128)
    dma = pltpu.SemaphoreType.DMA
    vmem = pltpu.VMEM
    scratch = [
        vmem((7200, 128), BF16),
        vmem((7264, 128), F32),
        vmem((2, NQ, ROWS, 128), F32),
        vmem((NQ, ROWS, 128), F32),
        vmem((ROWS, NQ * KQ), BF16),
        vmem((32, 80, 128), BF16),
        vmem((64, 80, 128), BF16),
        vmem((NQ * KQ, 256), BF16),
        vmem((NQ * KQ, 256), BF16),
        vmem((32, 16, 128), F32),
        pltpu.SMEM((8, 128), I32),
        pltpu.SMEM((2, 48), I32),
        vmem((16, 2, 24, 128), F32),
        vmem((16, 2, 24, 128), F32),
        vmem((2, 24, 128), F32),
        vmem((8, 8, 128), F32),
        vmem((16, 8, 128), F32),
        vmem((16, 128), F32),
        dma((4,)),
        dma((9,)),
    ]
    scratch += [dma((8,))] * 10 + [dma((16,))] * 4
    return pl.pallas_call(
        kernel,
        out_shape=jax.ShapeDtypeStruct((6, 128), F32),
        in_specs=[pl.BlockSpec(memory_space=pl.ANY)] * 5,
        out_specs=pl.BlockSpec(memory_space=pltpu.VMEM),
        scratch_shapes=scratch,
        compiler_params=pltpu.CompilerParams(
            collective_id=0, has_side_effects=True, vmem_limit_bytes=48 * 1024 * 1024
        ),
    )(propagator, rows, momentum_shift, frequency_shift, jnp.asarray(minus_functions()))


def solution(mesh):
    from jax.sharding import PartitionSpec as P

    in_specs = (P(None, "pb"), P("pb", "wa", None), P("pb", None), P("wa", None))
    out_specs = P("wa", "pb")
    return jax.shard_map(local, mesh=mesh, in_specs=in_specs, out_specs=out_specs, check_vma=False)
```

time: 835 us -> 49.9 us (0.06)
  local copies, waits for them, and re-layouts: 312 us -> 5.36 us
  waiting for transfers between devices: 264 us -> 0 us
  other arithmetic: 141 us -> 0 us
  blocking collectives: 72.7 us -> 0 us
  Pallas kernels: 0 us -> 44.3 us
  matrix products: 26.1 us -> 0 us
  between operations: 13.4 us -> 0.01 us
    unnamed x2 -> x0, waiting for transfers between devices: 264 us -> none
    gather x32 -> x0, local copies, waits for them, and re-layouts: 253 us -> none  [the longest x16 240 us: pair_flow(): shifted = jnp.take(selected, shift_row, axis=1).astype(jnp.float32)]
    convert_element_type x32 -> x0, other arithmetic: 74.4 us -> none  [the longest x16 53.9 us: pair_flow(): shifted = jnp.take(selected, shift_row, axis=1).astype(jnp.float32)]
    all_gather x1 -> x0, blocking collectives: 72.7 us -> none  [local(): gathered = lax.all_gather(propagator, 'pb', axis=1, tiled=True)]
    pallas_call x0 -> x1, Pallas kernels: none -> 44.3 us  [local(): pl.pallas_call(kernel, out_shape=jax.ShapeDtypeStruct((6, 128), F32), in_...]
    add x16 -> x0, other arithmetic: 33.1 us -> none  [accumulate(): return total + term]
    select_n x48 -> x0, other arithmetic: 28.8 us -> none  [the longest x16 15 us: pair_flow(): shifted = jnp.take(selected, shift_row, axis=1).astype(jnp.float32)]
    dynamic_slice x16 -> x0, local copies, waits for them, and re-layouts: 26.1 us -> none  [accumulate(): vertex[q_index, w_index]]
  transfers between devices with their start and end apart: 1 -> 0, of which waited for: 1 -> 0; matrix products, arithmetic and copies ran while one was open for 0% -> 0% of each run, Pallas kernels for 0% -> 0%
where the time goes in v1:
time: 49.9 us; the launch traced here: 49.6 us
  Pallas kernels  44.3 us (89%)
  local copies, waits for them, and re-layouts  5.36 us (11%)
    pallas_call x1, Pallas kernels, local(): pl.pallas_call(kernel, out_shape=jax.ShapeDtypeStruct((6, 128), F32), in_...  44.3 us
    unnamed x11, local copies, waits for them, and re-layouts  5.36 us

profile of v1, /device:TPU:1, one launch (start us, length us, event | category | flops | bytes accessed | tf_op | source)
XLA Modules:
  0.0 49.6 jit_solution(5266623985048611742)
XLA Ops:
  0.0 0.0 copy-start
  0.0 1.5 %copy-done = bf16[8,2,57600]{2,1,0:T(2,128)(2,1)S(1)} copy-done((bf16[8,2,57600]{2,1,0:T(2,128)(2,1)S(1)}, bf16[8,2,57600]{2,1,0:T(2,128)(2,1)}, u32[]{:S(2)}) %copy-start) | copy-done | bytes 1843224
  1.5 0.0 copy-start.1
  1.5 0.9 %copy-done.1 = f32[32,16,128]{2,1,0:T(8,128)S(1)} copy-done((f32[32,16,128]{2,1,0:T(8,128)S(1)}, f32[32,16,128]{2,1,0:T(8,128)}, u32[]{:S(2)}) %copy-start.1) | copy-done | bytes 262168
  2.5 0.0 copy-start.2
  2.5 0.9 %copy-done.2 = s32[8,4096]{1,0:T(8,128)S(1)} copy-done((s32[8,4096]{1,0:T(8,128)S(1)}, s32[8,4096]{1,0:T(8,128)}, u32[]{:S(2)}) %copy-start.2) | copy-done | bytes 131096
  3.4 0.0 copy-start.3
  3.4 0.7 %copy-done.3 = bf16[80,128]{1,0:T(8,128)(2,1)S(1)} copy-done((bf16[80,128]{1,0:T(8,128)(2,1)S(1)}, bf16[80,128]{1,0:T(8,128)(2,1)}, u32[]{:S(2)}) %copy-start.3) | copy-done | bytes 20504
  4.1 0.0 copy-start.4
  4.1 0.7 %copy-done.4 = s32[2,48]{1,0:T(2,128)S(1)} copy-done((s32[2,48]{1,0:T(2,128)S(1)}, s32[2,48]{1,0:T(2,128)}, u32[]{:S(2)}) %copy-start.4) | copy-done | bytes 408
  4.8 44.3 %shard_map.55 = f32[6,128]{1,0:T(8,128)S(1)} custom-call(bf16[80,128]{1,0:T(8,128)(2,1)S(1)} %copy-done.3, bf16[7200,128]{1,0:T(8,128)(2,1)S(1)} %bitcast.7, s32[8,4096]{1,0:T(8,128)S(1)} %copy-done.2, s32[2,48]{1,0:T(2,128)S(1)} %copy-done.4, f32[32,16,128]{2,1,0:T(8,128)S(1)} %copy-done.1), custom_call_target="tpu_custom_call" | custom-call | tf_op jit(solution)/shard_map/pallas_call | solution.py:390
  49.0 0.6 %copy.7 = f32[6,128]{1,0:T(8,128)} copy(f32[6,128]{1,0:T(8,128)S(1)} %shard_map.55) | data formatting | bytes 6144
Async XLA Ops:
  0.0 1.5 %copy-start = (bf16[8,2,57600]{2,1,0:T(2,128)(2,1)S(1)}, bf16[8,2,57600]{2,1,0:T(2,128)(2,1)}, u32[]{:S(2)}) copy-start(bf16[8,2,57600]{2,1,0:T(2,128)(2,1)} %param.6) | copy-start | bytes 5529604
  1.5 0.9 %copy-start.1 = (f32[32,16,128]{2,1,0:T(8,128)S(1)}, f32[32,16,128]{2,1,0:T(8,128)}, u32[]{:S(2)}) copy-start(f32[32,16,128]{2,1,0:T(8,128)} %constant.2.clone.table) | copy-start | bytes 786436
  2.5 0.9 %copy-start.2 = (s32[8,4096]{1,0:T(8,128)S(1)}, s32[8,4096]{1,0:T(8,128)}, u32[]{:S(2)}) copy-start(s32[8,4096]{1,0:T(8,128)} %mom.1) | copy-start | bytes 393220
  3.4 0.7 %copy-start.3 = (bf16[80,128]{1,0:T(8,128)(2,1)S(1)}, bf16[80,128]{1,0:T(8,128)(2,1)}, u32[]{:S(2)}) copy-start(bf16[80,128]{1,0:T(8,128)(2,1)} %prop.1) | copy-start | bytes 61444
  4.1 0.7 %copy-start.4 = (s32[2,48]{1,0:T(2,128)S(1)}, s32[2,48]{1,0:T(2,128)}, u32[]{:S(2)}) copy-start(s32[2,48]{1,0:T(2,128)} %freq.1) | copy-start | bytes 1156

commit v2 on v1

v2 whole, which is shorter than its diff:
```python
import math

import jax
import jax.numpy as jnp
import numpy as np
from jax import lax
from jax.experimental import pallas as pl
from jax.experimental.pallas import tpu as pltpu

LAT = 64
F32 = jnp.float32
BF16 = jnp.bfloat16
I32 = jnp.int32
NQ = 8
NB = 13
ROWS = NB * 48
KQ = 80
DIST = (0, 1, 2, 1)

OFFSETS = sorted(
    ((a, y, x) for a in range(2) for y in range(4) for x in range(4) if a + y + x),
    key=lambda o: -(o[0] + DIST[o[1]] + DIST[o[2]]),
)
EVEN = [o for o in OFFSETS if sum(o) % 2 == 0]
ODD = [o for o in OFFSETS if sum(o) % 2 == 1]

BLOCKS = (
    ((0, 0, 1), (1, 1, 1), (2, 2, 1), (3, 3, 1), (4, 4, 1)),
    ((0, 1, 1), (1, 0, 1)),
    ((0, 2, 1), (2, 0, 1)),
    ((0, 3, 1), (3, 0, 1)),
    ((0, 4, 1), (4, 0, 1)),
    ((1, 1, 1), (3, 3, -1)),
    ((1, 3, 1), (3, 1, 1)),
    ((2, 2, 1), (4, 4, -1)),
    ((2, 4, 1), (4, 2, 1)),
    ((1, 2, 1), (2, 1, 1)),
    ((1, 4, 1), (4, 1, 1)),
    ((2, 3, 1), (3, 2, 1)),
    ((3, 4, 1), (4, 3, 1)),
)


def minus_functions():
    k = np.arange(LAT * LAT)
    a = (k // LAT) * (2.0 * math.pi / LAT)
    b = (k % LAT) * (2.0 * math.pi / LAT)
    root = math.sqrt(2.0)
    ca, cb, sa, sb = np.cos(a), np.cos(b), np.sin(a), np.sin(b)
    rows = [
        np.ones_like(a),
        root * ca,
        root * cb,
        root * sa,
        root * sb,
        np.cos(2 * a),
        np.sin(2 * a),
        np.cos(2 * b),
        np.sin(2 * b),
        2 * ca * cb,
        2 * ca * sb,
        2 * cb * sa,
        2 * sa * sb,
    ]
    table = np.zeros((16, LAT * LAT), np.float32)
    table[:NB] = -np.stack(rows)
    return np.ascontiguousarray(table.reshape(16, 32, 128).transpose(1, 0, 2))


def kernel(
    prop, vert, mom, freq, table, out,
    vb, s32, wown, wrecv, lhs, gs, dup, rhs0, rhs1, tab, momv, freqv,
    ssend, srecv, red, fsend, frecv,
    in_sem, v_sem, w_s, w_r, f_s, f_r, ag_s, ag_r, c_s, c_r, s_s, s_r,
):
    p = lax.axis_index("pb")
    wa = lax.axis_index("wa")
    zl = p // 16
    yy = (p // 4) % 4
    xx = p % 4
    core = wa % 2
    z = (wa // 2) * 2 + zl
    other = 1 - core
    sibling = (p, (wa // 2) * 2 + other)

    def remote(src, dst, send, recv, device):
        return pltpu.make_async_remote_copy(
            src_ref=src, dst_ref=dst, send_sem=send, recv_sem=recv,
            device_id=device, device_id_type=pl.DeviceIdType.MESH,
        )

    def signal(device):
        pl.semaphore_signal(barrier, inc=1, device_id=device, device_id_type=pl.DeviceIdType.MESH)

    def each(n, body):
        def step(i, carry):
            body(i)
            return carry

        lax.fori_loop(0, n, step, 0)

    def mixed(first, second, which):
        return tuple(a + (b - a) * which for a, b in zip(first, second))

    def pick(i, which):
        return mixed(EVEN[min(i, 14)], ODD[i], which)

    def slot(o, sign):
        a, y, x = o
        return ((zl + a) % 2) * 16 + ((yy + sign * y + 4) % 4) * 4 + (xx + sign * x + 4) % 4

    def plane(e, sign):
        return ((yy + sign * (e // 4) + 4) % 4) * 4 + (xx + sign * (e % 4) + 4) % 4

    def mate(o):
        zz = (z + o[0] * (1 - 2 * zl) + 8) % 8
        return (slot(o, 1), (zz // 2) * 2 + core)

    barrier = pltpu.get_barrier_semaphore()
    for i in range(15):
        signal(mate(pick(i, core)))

    @pl.when(core == 1)
    def _():
        signal(mate(ODD[15]))

    plane_even = [o for o in EVEN if o[0] == 0]
    plane_odd = [o for o in ODD if o[0] == 0]
    for i in range(7):
        signal(mate(mixed(plane_odd[i], plane_even[i], core)))

    @pl.when(core == 0)
    def _():
        signal(mate(plane_odd[7]))

    for d in range(1, 8):
        zz = (z + d) % 8
        signal(((zz % 2) * 16 + p % 16, (zz // 2) * 2 + zl))

    @pl.when(core != zl)
    def _():
        signal(sibling)

    signal(sibling)

    c_mom = pltpu.make_async_copy(mom.at[:, pl.ds(0, 128)], momv, in_sem.at[0])
    c_freq = pltpu.make_async_copy(freq, freqv, in_sem.at[1])
    c_tab = pltpu.make_async_copy(table.at[pl.ds(core * 16, 16)], tab, in_sem.at[2])
    c_own = pltpu.make_async_copy(prop, gs.at[p], in_sem.at[3])
    c_freq.start()

    def piece(i):
        rows = pl.ds(pl.multiple_of(i * 800, 800), 800)
        return pltpu.make_async_copy(vert.at[rows], vb.at[rows], v_sem.at[i])

    each(9, lambda i: piece(i).start())
    c_mom.start()
    c_own.start()
    c_tab.start()

    def widen(i):
        piece(i).wait()
        for t in range(5):
            rows = pl.ds(pl.multiple_of(i * 800 + t * 160, 160), 160)
            s32[rows, :] = vb[rows, :].astype(F32)

    each(9, widen)
    s32[pl.ds(7200, 64), :] = jnp.zeros((64, 128), F32)

    lane = lax.broadcasted_iota(I32, (8, 128), 1)
    c_freq.wait()

    def prepare(q):
        place = [(KQ * q) % 128 + freqv[w, 0] for w in range(2)]
        valid = [(lane + 256 - o) % 128 < 48 for o in place]
        for i in range(8):
            total = [None] * NB
            for w in range(2):
                blocks = {}
                for n2 in range(5):
                    off = 240 * i + 48 * n2
                    s, start = off // 128, off % 128
                    amount = (place[w] + (128 - start)) % 128
                    for n in range(5):
                        row = q * 900 + 180 * n + w + 2 * s
                        value = s32[pl.ds(row, 8, stride=30), :]
                        if start > 80:
                            after = s32[pl.ds(row + 2, 8, stride=30), :]
                            value = jnp.where(lane < start, after, value)
                        blocks[n, n2] = pltpu.roll(value, amount, 1)
                for f in range(NB):
                    term = None
                    for n, n2, sign in BLOCKS[f]:
                        if term is None:
                            term = blocks[n, n2]
                        elif sign > 0:
                            term = term + blocks[n, n2]
                        else:
                            term = term - blocks[n, n2]
                    term = jnp.where(valid[w], term, 0.0)
                    total[f] = term if total[f] is None else total[f] + term
            for f in range(NB):
                wown[q, pl.ds(48 * f + i, 6, stride=8), :] = total[f][0:6]

    each(NQ, prepare)
    c_own.wait()
    pl.semaphore_wait(barrier, 31 + core + zl - 2 * core * zl)

    def guard(i, which, body):
        if i < 15:
            body()
        else:
            pl.when(which == 1)(body)

    def ag(i):
        return remote(prop, gs.at[p], ag_s.at[i], ag_r.at[i], mate(pick(i, core)))

    def w_copy(q):
        return remote(wown.at[q], wrecv.at[q], w_s.at[q], w_r.at[q], sibling)

    def hand_on(i, which):
        block = slot(pick(i, which), -1)
        return remote(gs.at[block], gs.at[block], c_s.at[i], c_r.at[i], sibling)

    low = lax.broadcasted_iota(I32, (80, 128), 1) < 64

    def double(b):
        value = gs[b]
        turned = pltpu.roll(value, 64, 1)
        dup[2 * b] = jnp.where(low, value, turned)
        dup[2 * b + 1] = jnp.where(low, turned, value)

    for i in range(16):
        guard(i, core, lambda: ag(i).start())
    each(NQ, lambda q: w_copy(q).start())
    double(p)
    for i in reversed(range(16)):

        def pass_on():
            ag(i).wait_recv()
            hand_on(i, core).start()

        guard(i, core, pass_on)

    def settle(q):
        w_copy(q).wait_recv()

    each(NQ, settle)
    wide = lax.broadcasted_iota(I32, (48, 128), 1)

    def assemble(f):
        rows = pl.ds(pl.multiple_of(48 * f, 48), 48)
        tiles = [wown[q, rows, :] + wrecv[q, rows, :] for q in range(NQ)]
        for c in range(5):
            value = None
            for q in range(NQ):
                begin, end = KQ * q - 128 * c, KQ * (q + 1) - 128 * c
                if end <= 0 or begin >= 128:
                    continue
                value = tiles[q] if value is None else jnp.where(wide < begin, value, tiles[q])
            lhs[rows, 128 * c : 128 * c + 128] = value.astype(BF16)

    each(NB, assemble)
    for i in reversed(range(16)):
        guard(i, core, lambda: double(slot(pick(i, core), -1)))
    for i in reversed(range(16)):

        def receive():
            hand_on(i, other).wait_recv()
            double(slot(pick(i, other), -1))

        guard(i, other, receive)
    c_mom.wait()
    c_tab.wait()

    def build(step, ref):
        for half in range(2):
            x = 2 * (16 * core + plane(15 - 2 * step - half, 1))
            for q in range(NQ):
                shift = momv[q, 0]
                qx = shift // 64
                amount = (128 - shift % 64) % 128
                first = pltpu.roll(dup[(x + qx) % 64], amount, 1)
                second = pltpu.roll(dup[(x + 1 + qx) % 64], amount, 1)
                ref[KQ * q : KQ * q + 80, 128 * half : 128 * half + 128] = jnp.where(low, first, second)

    def s_copy(e):
        return remote(ssend.at[e], srecv.at[e], s_s.at[e], s_r.at[e], (zl * 16 + plane(e, 1), wa))

    def contract(step, ref):
        acc = jnp.dot(lhs[...], ref[...], preferred_element_type=F32)
        for half in range(2):
            e = 15 - 2 * step - half
            factors = tab[plane(e, 1)]
            flow = None
            for f in range(NB):
                term = factors[f : f + 1, :] * acc[48 * f : 48 * f + 48, 128 * half : 128 * half + 128]
                flow = term if flow is None else flow + term
            ssend[e] = flow

            @pl.when(e != 0)
            def _():
                s_copy(e).start()

    build(0, rhs0)

    def two(i):
        build(2 * i + 1, rhs1)
        contract(2 * i, rhs0)
        build((2 * i + 2) % 8, rhs0)
        contract(2 * i + 1, rhs1)

    each(4, two)

    red[...] = ssend[0]

    def gather_sum(i):
        e = 15 - i
        s_copy(e).wait_recv()
        red[...] += srecv[e]

    each(15, gather_sum)

    def f_copy(d):
        owner = 2 * ((wa // 2 + d // 2) % 4) + (core + d) % 2
        return remote(fsend.at[owner], frecv.at[z], f_s.at[d], f_r.at[z], (core * 16 + p % 16, owner))

    def f_arrival(d):
        k = (z + d) % 8
        return remote(fsend.at[0], frecv.at[k], f_s.at[0], f_r.at[k], ((k % 2) * 16 + p % 16, (k // 2) * 2 + zl))

    for j in range(8):
        fsend[j, 0:6, :] = red[6 * j : 6 * j + 6, :]
    for d in (4, 5, 2, 3, 6, 7, 1):
        f_copy(d).start()

    @pl.when(core != zl)
    def _():
        f_copy(0).start()
        f_arrival(0).wait_recv()

    @pl.when(core == zl)
    def _():
        frecv[z] = fsend[wa]

    for d in (1, 7, 2, 6, 3, 5, 4):
        f_arrival(d).wait_recv()
    total = frecv[0]
    for k in range(1, 8):
        total = total + frecv[k]
    out[...] = total[0:6]

    for i in range(16):

        def drain():
            ag(i).wait_send()
            hand_on(i, core).wait_send()

        guard(i, core, drain)
    each(NQ, lambda q: w_copy(q).wait_send())
    each(15, lambda i: s_copy(i + 1).wait_send())
    for d in range(1, 8):
        f_copy(d).wait_send()

    @pl.when(core != zl)
    def _():
        f_copy(0).wait_send()


def local(propagator, vertex, momentum_shift, frequency_shift):
    rows = vertex.transpose(0, 2, 1).reshape(3600, 128, 2).transpose(0, 2, 1).reshape(7200, 128)
    dma = pltpu.SemaphoreType.DMA
    vmem = pltpu.VMEM
    scratch = [
        vmem((7200, 128), BF16),
        vmem((7264, 128), F32),
        vmem((NQ, ROWS, 128), F32),
        vmem((NQ, ROWS, 128), F32),
        vmem((ROWS, NQ * KQ), BF16),
        vmem((32, 80, 128), BF16),
        vmem((64, 80, 128), BF16),
        vmem((NQ * KQ, 256), BF16),
        vmem((NQ * KQ, 256), BF16),
        vmem((16, 16, 128), F32),
        pltpu.SMEM((8, 128), I32),
        pltpu.SMEM((2, 48), I32),
        vmem((16, 48, 128), F32),
        vmem((16, 48, 128), F32),
        vmem((48, 128), F32),
        vmem((8, 8, 128), F32),
        vmem((8, 8, 128), F32),
        dma((4,)),
        dma((9,)),
    ]
    scratch += [dma((8,))] * 4 + [dma((16,))] * 6
    return pl.pallas_call(
        kernel,
        out_shape=jax.ShapeDtypeStruct((6, 128), F32),
        in_specs=[pl.BlockSpec(memory_space=pltpu.HBM)] * 5,
        out_specs=pl.BlockSpec(memory_space=pltpu.VMEM),
        scratch_shapes=scratch,
        compiler_params=pltpu.CompilerParams(
            collective_id=0, has_side_effects=True, vmem_limit_bytes=62 * 1024 * 1024
        ),
    )(propagator, rows, momentum_shift, frequency_shift, jnp.asarray(minus_functions()))


def solution(mesh):
    from jax.sharding import PartitionSpec as P

    in_specs = (P(None, "pb"), P("pb", "wa", None), P("pb", None), P("wa", None))
    out_specs = P("wa", "pb")
    return jax.shard_map(local, mesh=mesh, in_specs=in_specs, out_specs=out_specs, check_vma=False)
```

time: 49.9 us -> 40.3 us (0.81)
  Pallas kernels: 44.3 us -> 38.9 us
  local copies, waits for them, and re-layouts: 5.36 us -> 1.28 us
    pallas_call x1, Pallas kernels: 44.3 us -> 38.9 us  [local(): pl.pallas_call(kernel, out_shape=jax.ShapeDtypeStruct((6, 128), F32), in_...]
    unnamed x11 -> x1, local copies, waits for them, and re-layouts: 5.36 us -> 1.28 us
where the time goes in v2:
time: 40.3 us; the launch traced here: 40.2 us
  Pallas kernels  38.9 us (97%)
  local copies, waits for them, and re-layouts  1.28 us (3%)
    pallas_call x1, Pallas kernels, local(): pl.pallas_call(kernel, out_shape=jax.ShapeDtypeStruct((6, 128), F32), in_...  38.9 us
    unnamed x1, local copies, waits for them, and re-layouts  1.28 us

profile of v2, /device:TPU:1, one launch (start us, length us, event | category | flops | bytes accessed | tf_op | source)
XLA Modules:
  0.0 40.2 jit_solution(7204295728756145975)
XLA Ops:
  0.0 38.9 %shard_map.55 = f32[6,128]{1,0:T(8,128)} custom-call(bf16[80,128]{1,0:T(8,128)(2,1)} %prop.1, bf16[7200,128]{1,0:T(8,128)(2,1)} %bitcast.7, s32[8,4096]{1,0:T(8,128)} %mom.1, s32[2,48]{1,0:T(2,128)} %freq.1, f32[32,16,128]{2,1,0:T(8,128)} %constant.2.clone.table), custom_call_target="tpu_custom_call" | custom-call | tf_op jit(solution)/shard_map/pallas_call | solution.py:396
  38.9 1.3 %copy.7 = f32[6,128]{1,0:T(8,128)} copy(f32[6,128]{1,0:T(8,128)} %shard_map.55) | data formatting | bytes 6144

commit v3 on v2

--- a/solution.py
+++ b/solution.py
@@ -16,6 +16,7 @@
 ROWS = NB * 48
 KQ = 80
 DIST = (0, 1, 2, 1)
+ORDER = (10, 9, 11, 6, 14, 8, 2, 5, 7, 13, 15, 1, 3, 4, 12, 0)
 
 OFFSETS = sorted(
     ((a, y, x) for a in range(2) for y in range(4) for x in range(4) if a + y + x),
@@ -202,7 +203,6 @@
             for f in range(NB):
                 wown[q, pl.ds(48 * f + i, 6, stride=8), :] = total[f][0:6]
 
-    each(NQ, prepare)
     c_own.wait()
     pl.semaphore_wait(barrier, 31 + core + zl - 2 * core * zl)
 
@@ -232,7 +232,12 @@
 
     for i in range(16):
         guard(i, core, lambda: ag(i).start())
-    each(NQ, lambda q: w_copy(q).start())
+
+    def prepare_and_send(q):
+        prepare(q)
+        w_copy(q).start()
+
+    each(NQ, prepare_and_send)
     double(p)
     for i in reversed(range(16)):
 
@@ -273,53 +278,46 @@
     c_mom.wait()
     c_tab.wait()
 
-    def build(step, ref):
-        for half in range(2):
-            x = 2 * (16 * core + plane(15 - 2 * step - half, 1))
+    def build(step):
+        ref = rhs[step % 2]
+        for part in range(4):
+            x = 2 * (16 * core + plane(ORDER[4 * step + part], 1))
             for q in range(NQ):
                 shift = momv[q, 0]
                 qx = shift // 64
                 amount = (128 - shift % 64) % 128
                 first = pltpu.roll(dup[(x + qx) % 64], amount, 1)
                 second = pltpu.roll(dup[(x + 1 + qx) % 64], amount, 1)
-                ref[KQ * q : KQ * q + 80, 128 * half : 128 * half + 128] = jnp.where(low, first, second)
+                ref[KQ * q : KQ * q + 80, 128 * part : 128 * part + 128] = jnp.where(low, first, second)
 
     def s_copy(e):
         return remote(ssend.at[e], srecv.at[e], s_s.at[e], s_r.at[e], (zl * 16 + plane(e, 1), wa))
 
-    def contract(step, ref):
-        acc = jnp.dot(lhs[...], ref[...], preferred_element_type=F32)
-        for half in range(2):
-            e = 15 - 2 * step - half
+    def contract(step):
+        acc = jnp.dot(lhs[...], rhs[step % 2][...], preferred_element_type=F32)
+        for part in range(4):
+            e = ORDER[4 * step + part]
             factors = tab[plane(e, 1)]
             flow = None
             for f in range(NB):
-                term = factors[f : f + 1, :] * acc[48 * f : 48 * f + 48, 128 * half : 128 * half + 128]
+                term = factors[f : f + 1, :] * acc[48 * f : 48 * f + 48, 128 * part : 128 * part + 128]
                 flow = term if flow is None else flow + term
             ssend[e] = flow
-
-            @pl.when(e != 0)
-            def _():
+            if e:
                 s_copy(e).start()
 
-    build(0, rhs0)
-
-    def two(i):
-        build(2 * i + 1, rhs1)
-        contract(2 * i, rhs0)
-        build((2 * i + 2) % 8, rhs0)
-        contract(2 * i + 1, rhs1)
-
-    each(4, two)
+    rhs = (rhs0, rhs1)
+    build(0)
+    for step in range(4):
+        if step < 3:
+            build(step + 1)
+        contract(step)
 
     red[...] = ssend[0]
 
-    def gather_sum(i):
-        e = 15 - i
+    for e in ORDER[:15]:
         s_copy(e).wait_recv()
         red[...] += srecv[e]
-
-    each(15, gather_sum)
 
     def f_copy(d):
         owner = 2 * ((wa // 2 + d // 2) % 4) + (core + d) % 2
@@ -342,29 +340,29 @@
     @pl.when(core == zl)
     def _():
         frecv[z] = fsend[wa]
+
+    for i in range(16):
+
+        def drain():
+            ag(i).wait_send()
+            hand_on(i, core).wait_send()
+
+        guard(i, core, drain)
+    each(NQ, lambda q: w_copy(q).wait_send())
+    each(15, lambda i: s_copy(i + 1).wait_send())
 
     for d in (1, 7, 2, 6, 3, 5, 4):
         f_arrival(d).wait_recv()
     total = frecv[0]
     for k in range(1, 8):
         total = total + frecv[k]
-    out[...] = total[0:6]
-
-    for i in range(16):
-
-        def drain():
-            ag(i).wait_send()
-            hand_on(i, core).wait_send()
-
-        guard(i, core, drain)
-    each(NQ, lambda q: w_copy(q).wait_send())
-    each(15, lambda i: s_copy(i + 1).wait_send())
     for d in range(1, 8):
         f_copy(d).wait_send()
 
     @pl.when(core != zl)
     def _():
         f_copy(0).wait_send()
+    out[...] = total[0:6]
 
 
 def local(propagator, vertex, momentum_shift, frequency_shift):
@@ -379,8 +377,8 @@
         vmem((ROWS, NQ * KQ), BF16),
         vmem((32, 80, 128), BF16),
         vmem((64, 80, 128), BF16),
-        vmem((NQ * KQ, 256), BF16),
-        vmem((NQ * KQ, 256), BF16),
+        vmem((NQ * KQ, 512), BF16),
+        vmem((NQ * KQ, 512), BF16),
         vmem((16, 16, 128), F32),
         pltpu.SMEM((8, 128), I32),
         pltpu.SMEM((2, 48), I32),
@@ -400,7 +398,7 @@
         out_specs=pl.BlockSpec(memory_space=pltpu.VMEM),
         scratch_shapes=scratch,
         compiler_params=pltpu.CompilerParams(
-            collective_id=0, has_side_effects=True, vmem_limit_bytes=62 * 1024 * 1024
+            collective_id=0, has_side_effects=True, vmem_limit_bytes=56549376
         ),
     )(propagator, rows, momentum_shift, frequency_shift, jnp.asarray(minus_functions()))
 

time: 40.3 us -> 35.7 us (0.89)
  Pallas kernels: 38.9 us -> 34.3 us
    pallas_call x1, Pallas kernels: 38.9 us -> 34.3 us  [local(): pl.pallas_call(kernel, out_shape=jax.ShapeDtypeStruct((6, 128), F32), in_...]
    unnamed x1 -> x3, local copies, waits for them, and re-layouts: 1.28 us -> 1.27 us
where the time goes in v3:
time: 35.7 us; the launch traced here: 35.6 us
  Pallas kernels  34.3 us (96%)
  local copies, waits for them, and re-layouts  1.27 us (4%)
    pallas_call x1, Pallas kernels, local(): pl.pallas_call(kernel, out_shape=jax.ShapeDtypeStruct((6, 128), F32), in_...  34.3 us
    unnamed x3, local copies, waits for them, and re-layouts  1.27 us

profile of v3, /device:TPU:1, one launch (start us, length us, event | category | flops | bytes accessed | tf_op | source)
XLA Modules:
  0.0 35.6 jit_solution(2087406424248313459)
XLA Ops:
  0.0 0.0 copy-start
  0.0 0.7 %copy-done = s32[2,48]{1,0:T(2,128)S(1)} copy-done((s32[2,48]{1,0:T(2,128)S(1)}, s32[2,48]{1,0:T(2,128)}, u32[]{:S(2)}) %copy-start) | copy-done | bytes 408
  0.7 34.3 %shard_map.55 = f32[6,128]{1,0:T(8,128)S(1)} custom-call(bf16[80,128]{1,0:T(8,128)(2,1)} %prop.1, bf16[7200,128]{1,0:T(8,128)(2,1)} %bitcast.7, s32[8,4096]{1,0:T(8,128)} %mom.1, s32[2,48]{1,0:T(2,128)S(1)} %copy-done, f32[32,16,128]{2,1,0:T(8,128)} %constant.2.clone.table), custom_call_target="tpu_custom_call" | custom-call | tf_op jit(solution)/shard_map/pallas_call | solution.py:394
  35.0 0.6 %copy.7 = f32[6,128]{1,0:T(8,128)} copy(f32[6,128]{1,0:T(8,128)S(1)} %shard_map.55) | data formatting | bytes 6144
Async XLA Ops:
  0.0 0.7 %copy-start = (s32[2,48]{1,0:T(2,128)S(1)}, s32[2,48]{1,0:T(2,128)}, u32[]{:S(2)}) copy-start(s32[2,48]{1,0:T(2,128)} %freq.1) | copy-start | bytes 1156

commit v4 on v3

--- a/solution.py
+++ b/solution.py
@@ -16,6 +16,7 @@
 ROWS = NB * 48
 KQ = 80
 DIST = (0, 1, 2, 1)
+BITS = 14.0
 ORDER = (10, 9, 11, 6, 14, 8, 2, 5, 7, 13, 15, 1, 3, 4, 12, 0)
 
 OFFSETS = sorted(
@@ -290,6 +291,21 @@
                 second = pltpu.roll(dup[(x + 1 + qx) % 64], amount, 1)
                 ref[KQ * q : KQ * q + 80, 128 * part : 128 * part + 128] = jnp.where(low, first, second)
 
+    def encode(flow, ref):
+        top = jnp.abs(flow[0:8])
+        for t in range(1, 6):
+            top = jnp.maximum(top, jnp.abs(flow[8 * t : 8 * t + 8]))
+        power = jnp.floor(jnp.log2(jnp.maximum(top, 2.0**-100))) + 1.0
+        unit = jnp.exp2(BITS - power)
+        parts = [jnp.round(flow[8 * t : 8 * t + 8] * unit) for t in range(6)]
+        ref[...] = jnp.concatenate(parts + [power, power], axis=0).astype(I32).astype(jnp.int16)
+
+    def decode(ref):
+        values = ref[...].astype(I32).astype(F32)
+        unit = jnp.exp2(values[48:56] - BITS)
+        for t in range(6):
+            red[8 * t : 8 * t + 8, :] += values[8 * t : 8 * t + 8] * unit
+
     def s_copy(e):
         return remote(ssend.at[e], srecv.at[e], s_s.at[e], s_r.at[e], (zl * 16 + plane(e, 1), wa))
 
@@ -302,9 +318,11 @@
             for f in range(NB):
                 term = factors[f : f + 1, :] * acc[48 * f : 48 * f + 48, 128 * part : 128 * part + 128]
                 flow = term if flow is None else flow + term
-            ssend[e] = flow
             if e:
+                encode(flow, ssend.at[e])
                 s_copy(e).start()
+            else:
+                red[...] = flow
 
     rhs = (rhs0, rhs1)
     build(0)
@@ -313,11 +331,9 @@
             build(step + 1)
         contract(step)
 
-    red[...] = ssend[0]
-
     for e in ORDER[:15]:
         s_copy(e).wait_recv()
-        red[...] += srecv[e]
+        decode(srecv.at[e])
 
     def f_copy(d):
         owner = 2 * ((wa // 2 + d // 2) % 4) + (core + d) % 2
@@ -382,8 +398,8 @@
         vmem((16, 16, 128), F32),
         pltpu.SMEM((8, 128), I32),
         pltpu.SMEM((2, 48), I32),
-        vmem((16, 48, 128), F32),
-        vmem((16, 48, 128), F32),
+        vmem((16, 64, 128), jnp.int16),
+        vmem((16, 64, 128), jnp.int16),
         vmem((48, 128), F32),
         vmem((8, 8, 128), F32),
         vmem((8, 8, 128), F32),

time: 35.7 us -> 34.4 us (0.964)
  Pallas kernels: 34.3 us -> 33 us
    pallas_call x1, Pallas kernels: 34.3 us -> 33 us  [local(): pl.pallas_call(kernel, out_shape=jax.ShapeDtypeStruct((6, 128), F32), in_...]
where the time goes in v4:
time: 34.4 us; the launch traced here: 34.3 us
  Pallas kernels  33 us (96%)
  local copies, waits for them, and re-layouts  1.27 us (4%)
    pallas_call x1, Pallas kernels, local(): pl.pallas_call(kernel, out_shape=jax.ShapeDtypeStruct((6, 128), F32), in_...  33 us
    unnamed x3, local copies, waits for them, and re-layouts  1.27 us

profile of v4, /device:TPU:1, one launch (start us, length us, event | category | flops | bytes accessed | tf_op | source)
XLA Modules:
  0.0 34.3 jit_solution(14845171890400639101)
XLA Ops:
  0.0 0.0 copy-start
  0.0 0.7 %copy-done = s32[2,48]{1,0:T(2,128)S(1)} copy-done((s32[2,48]{1,0:T(2,128)S(1)}, s32[2,48]{1,0:T(2,128)}, u32[]{:S(2)}) %copy-start) | copy-done | bytes 408
  0.7 33.0 %shard_map.55 = f32[6,128]{1,0:T(8,128)S(1)} custom-call(bf16[80,128]{1,0:T(8,128)(2,1)} %prop.1, bf16[7200,128]{1,0:T(8,128)(2,1)} %bitcast.7, s32[8,4096]{1,0:T(8,128)} %mom.1, s32[2,48]{1,0:T(2,128)S(1)} %copy-done, f32[32,16,128]{2,1,0:T(8,128)} %constant.2.clone.table), custom_call_target="tpu_custom_call" | custom-call | tf_op jit(solution)/shard_map/pallas_call | solution.py:410
  33.7 0.6 %copy.7 = f32[6,128]{1,0:T(8,128)} copy(f32[6,128]{1,0:T(8,128)S(1)} %shard_map.55) | data formatting | bytes 6144
Async XLA Ops:
  0.0 0.7 %copy-start = (s32[2,48]{1,0:T(2,128)S(1)}, s32[2,48]{1,0:T(2,128)}, u32[]{:S(2)}) copy-start(s32[2,48]{1,0:T(2,128)} %freq.1) | copy-start | bytes 1156

commit v5 on v4

--- a/solution.py
+++ b/solution.py
@@ -15,16 +15,8 @@
 NB = 13
 ROWS = NB * 48
 KQ = 80
-DIST = (0, 1, 2, 1)
 BITS = 14.0
-ORDER = (10, 9, 11, 6, 14, 8, 2, 5, 7, 13, 15, 1, 3, 4, 12, 0)
-
-OFFSETS = sorted(
-    ((a, y, x) for a in range(2) for y in range(4) for x in range(4) if a + y + x),
-    key=lambda o: -(o[0] + DIST[o[1]] + DIST[o[2]]),
-)
-EVEN = [o for o in OFFSETS if sum(o) % 2 == 0]
-ODD = [o for o in OFFSETS if sum(o) % 2 == 1]
+ORDER = (10, 9, 11, 14, 6, 8, 2, 13, 7, 5, 15, 4, 12, 1, 3, 0)
 
 BLOCKS = (
     ((0, 0, 1), (1, 1, 1), (2, 2, 1), (3, 3, 1), (4, 4, 1)),
@@ -101,11 +93,10 @@
 
         lax.fori_loop(0, n, step, 0)
 
-    def mixed(first, second, which):
-        return tuple(a + (b - a) * which for a, b in zip(first, second))
-
     def pick(i, which):
-        return mixed(EVEN[min(i, 14)], ODD[i], which)
+        y = (i // 4 + 2) % 4
+        x = (i % 4 + 2) % 4
+        return ((which + y + x) % 2, y, x)
 
     def slot(o, sign):
         a, y, x = o
@@ -119,25 +110,25 @@
         return (slot(o, 1), (zz // 2) * 2 + core)
 
     barrier = pltpu.get_barrier_semaphore()
-    for i in range(15):
-        signal(mate(pick(i, core)))
-
-    @pl.when(core == 1)
-    def _():
-        signal(mate(ODD[15]))
-
-    plane_even = [o for o in EVEN if o[0] == 0]
-    plane_odd = [o for o in ODD if o[0] == 0]
-    for i in range(7):
-        signal(mate(mixed(plane_odd[i], plane_even[i], core)))
-
-    @pl.when(core == 0)
-    def _():
-        signal(mate(plane_odd[7]))
-
-    for d in range(1, 8):
-        zz = (z + d) % 8
+    def guard(i, which, body):
+        pl.when((i != 10) | (which == 1))(body)
+
+    each(16, lambda i: guard(i, core, lambda: signal(mate(pick(i, core)))))
+
+    def greet_along(d):
+        zz = (z + 1 + d) % 8
         signal(((zz % 2) * 16 + p % 16, (zz // 2) * 2 + zl))
+
+    def greet_plane(i):
+        y = (i // 2 + 2) % 4
+        x = 2 * (i % 2) + (y + core + 1) % 2
+
+        @pl.when(4 * y + x != 0)
+        def _():
+            signal(mate((0, y, x)))
+
+    each(7, greet_along)
+    each(8, greet_plane)
 
     @pl.when(core != zl)
     def _():
@@ -207,14 +198,8 @@
     c_own.wait()
     pl.semaphore_wait(barrier, 31 + core + zl - 2 * core * zl)
 
-    def guard(i, which, body):
-        if i < 15:
-            body()
-        else:
-            pl.when(which == 1)(body)
-
     def ag(i):
-        return remote(prop, gs.at[p], ag_s.at[i], ag_r.at[i], mate(pick(i, core)))
+        return remote(gs.at[p], gs.at[p], ag_s.at[i], ag_r.at[i], mate(pick(i, core)))
 
     def w_copy(q):
         return remote(wown.at[q], wrecv.at[q], w_s.at[q], w_r.at[q], sibling)
@@ -231,8 +216,7 @@
         dup[2 * b] = jnp.where(low, value, turned)
         dup[2 * b + 1] = jnp.where(low, turned, value)
 
-    for i in range(16):
-        guard(i, core, lambda: ag(i).start())
+    each(16, lambda i: guard(i, core, lambda: ag(i).start()))
 
     def prepare_and_send(q):
         prepare(q)
@@ -240,13 +224,16 @@
 
     each(NQ, prepare_and_send)
     double(p)
-    for i in reversed(range(16)):
-
-        def pass_on():
+    def pass_on(n):
+        i = 15 - n
+
+        def body():
             ag(i).wait_recv()
             hand_on(i, core).start()
 
-        guard(i, core, pass_on)
+        guard(i, core, body)
+
+    each(16, pass_on)
 
     def settle(q):
         w_copy(q).wait_recv()
@@ -267,15 +254,20 @@
             lhs[rows, 128 * c : 128 * c + 128] = value.astype(BF16)
 
     each(NB, assemble)
-    for i in reversed(range(16)):
-        guard(i, core, lambda: double(slot(pick(i, core), -1)))
-    for i in reversed(range(16)):
-
-        def receive():
-            hand_on(i, other).wait_recv()
-            double(slot(pick(i, other), -1))
-
-        guard(i, other, receive)
+    def double_own(n):
+        for u in range(4):
+            double(slot(pick(4 * n + u, core), -1))
+
+    each(4, double_own)
+
+    def receive(n):
+        for u in range(4):
+            i = 15 - 4 * n - u
+            guard(i, other, hand_on(i, other).wait_recv)
+        for u in range(4):
+            double(slot(pick(15 - 4 * n - u, other), -1))
+
+    each(4, receive)
     c_mom.wait()
     c_tab.wait()
 
@@ -303,8 +295,7 @@
     def decode(ref):
         values = ref[...].astype(I32).astype(F32)
         unit = jnp.exp2(values[48:56] - BITS)
-        for t in range(6):
-            red[8 * t : 8 * t + 8, :] += values[8 * t : 8 * t + 8] * unit
+        return jnp.concatenate([values[8 * t : 8 * t + 8] * unit for t in range(6)], axis=0)
 
     def s_copy(e):
         return remote(ssend.at[e], srecv.at[e], s_s.at[e], s_r.at[e], (zl * 16 + plane(e, 1), wa))
@@ -320,9 +311,11 @@
                 flow = term if flow is None else flow + term
             if e:
                 encode(flow, ssend.at[e])
-                s_copy(e).start()
             else:
                 red[...] = flow
+        for part in range(4):
+            if ORDER[4 * step + part]:
+                s_copy(ORDER[4 * step + part]).start()
 
     rhs = (rhs0, rhs1)
     build(0)
@@ -331,9 +324,13 @@
             build(step + 1)
         contract(step)
 
-    for e in ORDER[:15]:
-        s_copy(e).wait_recv()
-        decode(srecv.at[e])
+    for group in (ORDER[0:11], ORDER[11:15]):
+        for e in group:
+            s_copy(e).wait_recv()
+        flow = red[...]
+        for e in group:
+            flow = flow + decode(srecv.at[e])
+        red[...] = flow
 
     def f_copy(d):
         owner = 2 * ((wa // 2 + d // 2) % 4) + (core + d) % 2
@@ -357,27 +354,29 @@
     def _():
         frecv[z] = fsend[wa]
 
-    for i in range(16):
-
-        def drain():
+    def drain(i):
+        def body():
             ag(i).wait_send()
             hand_on(i, core).wait_send()
 
-        guard(i, core, drain)
+        guard(i, core, body)
+
+    each(16, drain)
     each(NQ, lambda q: w_copy(q).wait_send())
     each(15, lambda i: s_copy(i + 1).wait_send())
+
+    for d in range(1, 8):
+        f_copy(d).wait_send()
+
+    @pl.when(core != zl)
+    def _():
+        f_copy(0).wait_send()
 
     for d in (1, 7, 2, 6, 3, 5, 4):
         f_arrival(d).wait_recv()
     total = frecv[0]
     for k in range(1, 8):
         total = total + frecv[k]
-    for d in range(1, 8):
-        f_copy(d).wait_send()
-
-    @pl.when(core != zl)
-    def _():
-        f_copy(0).wait_send()
     out[...] = total[0:6]
 
 

time: 34.4 us -> 34 us (0.988)
  Pallas kernels: 33 us -> 32.6 us
    pallas_call x1, Pallas kernels: 33 us -> 32.6 us  [local(): pl.pallas_call(kernel, out_shape=jax.ShapeDtypeStruct((6, 128), F32), in_...]
where the time goes in v5:
time: 34 us; the launch traced here: 33.9 us
  Pallas kernels  32.6 us (96%)
  local copies, waits for them, and re-layouts  1.27 us (4%)
    pallas_call x1, Pallas kernels, local(): pl.pallas_call(kernel, out_shape=jax.ShapeDtypeStruct((6, 128), F32), in_...  32.6 us
    unnamed x3, local copies, waits for them, and re-layouts  1.27 us

profile of v5, /device:TPU:1, one launch (start us, length us, event | category | flops | bytes accessed | tf_op | source)
XLA Modules:
  0.0 33.9 jit_solution(14044812134044734690)
XLA Ops:
  0.0 0.0 copy-start
  0.0 0.7 %copy-done = s32[2,48]{1,0:T(2,128)S(1)} copy-done((s32[2,48]{1,0:T(2,128)S(1)}, s32[2,48]{1,0:T(2,128)}, u32[]{:S(2)}) %copy-start) | copy-done | bytes 408
  0.7 32.6 %shard_map.55 = f32[6,128]{1,0:T(8,128)S(1)} custom-call(bf16[80,128]{1,0:T(8,128)(2,1)} %prop.1, bf16[7200,128]{1,0:T(8,128)(2,1)} %bitcast.7, s32[8,4096]{1,0:T(8,128)} %mom.1, s32[2,48]{1,0:T(2,128)S(1)} %copy-done, f32[32,16,128]{2,1,0:T(8,128)} %constant.2.clone.table), custom_call_target="tpu_custom_call" | custom-call | tf_op jit(solution)/shard_map/pallas_call | solution.py:409
  33.3 0.6 %copy.7 = f32[6,128]{1,0:T(8,128)} copy(f32[6,128]{1,0:T(8,128)S(1)} %shard_map.55) | data formatting | bytes 6144
Async XLA Ops:
  0.0 0.7 %copy-start = (s32[2,48]{1,0:T(2,128)S(1)}, s32[2,48]{1,0:T(2,128)}, u32[]{:S(2)}) copy-start(s32[2,48]{1,0:T(2,128)} %freq.1) | copy-start | bytes 1156

commit v6 on v5

--- a/solution.py
+++ b/solution.py
@@ -202,7 +202,7 @@
         return remote(gs.at[p], gs.at[p], ag_s.at[i], ag_r.at[i], mate(pick(i, core)))
 
     def w_copy(q):
-        return remote(wown.at[q], wrecv.at[q], w_s.at[q], w_r.at[q], sibling)
+        return remote(wown.at[q, pl.ds(0, ROWS)], wrecv.at[q], w_s.at[q], w_r.at[q], sibling)
 
     def hand_on(i, which):
         block = slot(pick(i, which), -1)
@@ -312,7 +312,7 @@
             if e:
                 encode(flow, ssend.at[e])
             else:
-                red[...] = flow
+                red[0:48, :] = flow
         for part in range(4):
             if ORDER[4 * step + part]:
                 s_copy(ORDER[4 * step + part]).start()
@@ -327,10 +327,10 @@
     for group in (ORDER[0:11], ORDER[11:15]):
         for e in group:
             s_copy(e).wait_recv()
-        flow = red[...]
+        flow = red[0:48, :]
         for e in group:
             flow = flow + decode(srecv.at[e])
-        red[...] = flow
+        red[0:48, :] = flow
 
     def f_copy(d):
         owner = 2 * ((wa // 2 + d // 2) % 4) + (core + d) % 2
@@ -387,7 +387,7 @@
     scratch = [
         vmem((7200, 128), BF16),
         vmem((7264, 128), F32),
-        vmem((NQ, ROWS, 128), F32),
+        vmem((NQ, ROWS + 16, 128), F32),
         vmem((NQ, ROWS, 128), F32),
         vmem((ROWS, NQ * KQ), BF16),
         vmem((32, 80, 128), BF16),
@@ -399,7 +399,7 @@
         pltpu.SMEM((2, 48), I32),
         vmem((16, 64, 128), jnp.int16),
         vmem((16, 64, 128), jnp.int16),
-        vmem((48, 128), F32),
+        vmem((56, 128), F32),
         vmem((8, 8, 128), F32),
         vmem((8, 8, 128), F32),
         dma((4,)),

time: 34 us -> 34 us (level)
  no operation moved by 1% of the time
where the time goes in v6:
time: 34 us; the launch traced here: 33.8 us
  Pallas kernels  32.6 us (96%)
  local copies, waits for them, and re-layouts  1.27 us (4%)
    pallas_call x1, Pallas kernels, local(): pl.pallas_call(kernel, out_shape=jax.ShapeDtypeStruct((6, 128), F32), in_...  32.6 us
    unnamed x3, local copies, waits for them, and re-layouts  1.27 us

profile of v6, /device:TPU:1, one launch (start us, length us, event | category | flops | bytes accessed | tf_op | source)
XLA Modules:
  0.0 33.8 jit_solution(2799853421511091458)
XLA Ops:
  0.0 0.0 copy-start
  0.0 0.7 %copy-done = s32[2,48]{1,0:T(2,128)S(1)} copy-done((s32[2,48]{1,0:T(2,128)S(1)}, s32[2,48]{1,0:T(2,128)}, u32[]{:S(2)}) %copy-start) | copy-done | bytes 408
  0.7 32.6 %shard_map.55 = f32[6,128]{1,0:T(8,128)S(1)} custom-call(bf16[80,128]{1,0:T(8,128)(2,1)} %prop.1, bf16[7200,128]{1,0:T(8,128)(2,1)} %bitcast.7, s32[8,4096]{1,0:T(8,128)} %mom.1, s32[2,48]{1,0:T(2,128)S(1)} %copy-done, f32[32,16,128]{2,1,0:T(8,128)} %constant.2.clone.table), custom_call_target="tpu_custom_call" | custom-call | tf_op jit(solution)/shard_map/pallas_call | solution.py:409
  33.3 0.6 %copy.7 = f32[6,128]{1,0:T(8,128)} copy(f32[6,128]{1,0:T(8,128)S(1)} %shard_map.55) | data formatting | bytes 6144
Async XLA Ops:
  0.0 0.7 %copy-start = (s32[2,48]{1,0:T(2,128)S(1)}, s32[2,48]{1,0:T(2,128)}, u32[]{:S(2)}) copy-start(s32[2,48]{1,0:T(2,128)} %freq.1) | copy-start | bytes 1156

commit v7 on v6

--- a/solution.py
+++ b/solution.py
@@ -233,7 +233,7 @@
 
         guard(i, core, body)
 
-    each(16, pass_on)
+    each(8, pass_on)
 
     def settle(q):
         w_copy(q).wait_recv()
@@ -253,12 +253,14 @@
                 value = tiles[q] if value is None else jnp.where(wide < begin, value, tiles[q])
             lhs[rows, 128 * c : 128 * c + 128] = value.astype(BF16)
 
-    each(NB, assemble)
     def double_own(n):
         for u in range(4):
             double(slot(pick(4 * n + u, core), -1))
 
-    each(4, double_own)
+    each(NB, assemble)
+    each(2, lambda n: double_own(n + 2))
+    each(8, lambda n: pass_on(n + 8))
+    each(2, double_own)
 
     def receive(n):
         for u in range(4):

time: 34 us -> 34.1 us (level)
  no operation moved by 1% of the time
where the time goes in v7:
time: 34.1 us; the launch traced here: 34 us
  Pallas kernels  32.7 us (96%)
  local copies, waits for them, and re-layouts  1.27 us (4%)
    pallas_call x1, Pallas kernels, local(): pl.pallas_call(kernel, out_shape=jax.ShapeDtypeStruct((6, 128), F32), in_...  32.7 us
    unnamed x3, local copies, waits for them, and re-layouts  1.27 us

profile of v7, /device:TPU:1, one launch (start us, length us, event | category | flops | bytes accessed | tf_op | source)
XLA Modules:
  0.0 34.0 jit_solution(13054621892581427004)
XLA Ops:
  0.0 0.0 copy-start
  0.0 0.7 %copy-done = s32[2,48]{1,0:T(2,128)S(1)} copy-done((s32[2,48]{1,0:T(2,128)S(1)}, s32[2,48]{1,0:T(2,128)}, u32[]{:S(2)}) %copy-start) | copy-done | bytes 408
  0.7 32.7 %shard_map.55 = f32[6,128]{1,0:T(8,128)S(1)} custom-call(bf16[80,128]{1,0:T(8,128)(2,1)} %prop.1, bf16[7200,128]{1,0:T(8,128)(2,1)} %bitcast.7, s32[8,4096]{1,0:T(8,128)} %mom.1, s32[2,48]{1,0:T(2,128)S(1)} %copy-done, f32[32,16,128]{2,1,0:T(8,128)} %constant.2.clone.table), custom_call_target="tpu_custom_call" | custom-call | tf_op jit(solution)/shard_map/pallas_call | solution.py:411
  33.4 0.6 %copy.7 = f32[6,128]{1,0:T(8,128)} copy(f32[6,128]{1,0:T(8,128)S(1)} %shard_map.55) | data formatting | bytes 6144
Async XLA Ops:
  0.0 0.7 %copy-start = (s32[2,48]{1,0:T(2,128)S(1)}, s32[2,48]{1,0:T(2,128)}, u32[]{:S(2)}) copy-start(s32[2,48]{1,0:T(2,128)} %freq.1) | copy-start | bytes 1156
